TPU v7x, 32 devices: a whole 2x2x4 slice. The times are simulated.
32 devices in a mesh: groups: 2 (over x), expert: 16 (over z, y, core).
Axes of the slice: x: 2, y: 2, z: 4, core: 2. Of those that a mesh axis runs over, the one named last changes fastest.
Arguments:
- output_gradient: bfloat16 [2048, 8192], P('expert', 'groups'), parts along dimension 1, may hold values from -4 to 4
- router_weight_table: bfloat16 [2048, 16], P('expert', 'groups'), parts along dimension 1, may hold values from 0.019897461 to 0.5
- routes: int32 [2048, 16], P('expert', 'groups'), parts along dimension 1, may hold values from 0 to 15, all different within a row; in each aligned block of 128 rows (0 to 127, 128 to 255, ...) at most 72 rows name the same one
- hidden: bfloat16 [16, 2304, 768], P('expert', 'groups'), parts along dimension 1, may hold values from -4 to 4
- down_weight_matrix: bfloat16 [16, 768, 4096], P('expert'), may hold values from -0.21875 to 0.21875
- adapter_first_factor: bfloat16 [16, 768, 16], P('expert'), may hold values from -0.21875 to 0.21875
- adapter_second_factor: bfloat16 [16, 16, 4096], P('expert'), may hold values from -1.5 to 1.5
Outputs:
- hidden_input_gradient: bfloat16 [16, 2304, 768], P('expert', 'groups'), parts along dimension 1
- adapter_first_gradient: float32 [16, 1536, 16], P('expert', 'groups'), parts along dimension 1
- adapter_second_gradient: float32 [16, 32, 4096], P('expert', 'groups'), parts along dimension 1
- router_weight_gradient: float32 [2048, 16], P('expert', 'groups'), parts along dimension 1
There are 2 independent parts, one for each index of `groups`. A program takes and returns all parts, laid end to end along the dimension named above; an argument that names none is the same for every part. Nothing has to cross between parts.
Inputs may be any that keep to these rules, and one draw needn't show every extreme that they name: `routes`: each row names 8 different experts. Among the rows of one device no expert is named by more than 72 rows, and in some device's rows one expert is named by exactly 72.
All inputs are finite; a program needn't handle non-finite values.
Results may differ from a plain program's by a relative error of at most 0.0056.
Values may be sent and summed in bfloat16 or wider, within the bound.
A program may use at most 128 MiB of HBM per device.

v0:
```python
import jax
import jax.numpy as jnp
from jax import lax
from jax.sharding import PartitionSpec as P

adapter_scale = 2.0


def shards(
    output_gradient,
    router_weight_table,
    routes,
    hidden,
    down_weight_matrix,
    adapter_first_factor,
    adapter_second_factor,
):
    peer_count = lax.axis_size("expert")
    tokens_dev = output_gradient.shape[0]
    top_count = routes.shape[1]
    model_width = output_gradient.shape[1]
    exp_local = hidden.shape[0]
    capacity = hidden.shape[1]
    per_source = capacity // peer_count
    expert_count = exp_local * peer_count
    member = jnp.sum(
        (routes[:, :, None] == jnp.arange(expert_count, dtype=jnp.int32)).astype(jnp.bfloat16),
        axis=1,
    )
    lower_mask = (jnp.arange(tokens_dev)[:, None] > jnp.arange(tokens_dev)[None, :]).astype(
        jnp.bfloat16
    )
    before = jnp.dot(lower_mask, member, preferred_element_type=jnp.float32)
    position = jnp.take_along_axis(before, routes, axis=1).astype(jnp.int32)
    slot_index = (routes * per_source + position).reshape(-1)
    token_ids = jnp.repeat(jnp.arange(tokens_dev, dtype=jnp.int32), top_count)
    slot_token_index = (
        jnp.full((expert_count * per_source,), tokens_dev, jnp.int32).at[slot_index].set(token_ids)
    )
    slot_router_weight = (
        jnp.zeros((expert_count * per_source,), jnp.bfloat16)
        .at[slot_index]
        .set(router_weight_table.reshape(-1))
    )
    padded = jnp.concatenate(
        [output_gradient, jnp.zeros((1, model_width), output_gradient.dtype)], axis=0
    )
    send_rows = padded[slot_token_index]
    got_rows, got_weight = (
        lax.all_to_all(send_rows, "expert", split_axis=0, concat_axis=0, tiled=True),
        lax.all_to_all(slot_router_weight, "expert", split_axis=0, concat_axis=0, tiled=True),
    )
    slot_rows = (
        got_rows.reshape(peer_count, exp_local, per_source, model_width)
        .transpose(1, 0, 2, 3)
        .reshape(exp_local, capacity, model_width)
    )
    weight_rows = (
        got_weight.reshape(peer_count, exp_local, per_source)
        .transpose(1, 0, 2)
        .reshape(exp_local, capacity)
    )
    scaled_gradient = (
        weight_rows.astype(jnp.float32)[:, :, None] * slot_rows.astype(jnp.float32)
    ).astype(jnp.bfloat16)
    reduced_input = jnp.einsum(
        "onv,ovx->onx", hidden, adapter_first_factor, preferred_element_type=jnp.float32
    ).astype(jnp.bfloat16)
    joined_input = jnp.concatenate([hidden, reduced_input], axis=2)
    doubled_second = (adapter_scale * adapter_second_factor.astype(jnp.float32)).astype(
        jnp.bfloat16
    )
    joined_weight = jnp.concatenate([down_weight_matrix, doubled_second], axis=1)
    expert_out = jnp.einsum(
        "ecf,efd->ecd", joined_input, joined_weight, preferred_element_type=jnp.float32
    ).astype(jnp.bfloat16)
    partial_products = jnp.einsum(
        "ecd,ecd->ec", slot_rows, expert_out, preferred_element_type=jnp.float32
    )
    send_back = (
        partial_products.reshape(exp_local, peer_count, per_source).transpose(1, 0, 2).reshape(-1)
    )
    got_back = lax.all_to_all(send_back, "expert", split_axis=0, concat_axis=0, tiled=True)
    router_weight_gradient = got_back[slot_index].reshape(tokens_dev, top_count)
    reduced_gradient = jnp.einsum(
        "wzg,wvg->wzv", scaled_gradient, adapter_second_factor, preferred_element_type=jnp.float32
    ).astype(jnp.bfloat16)
    hidden_input_gradient = (
        jnp.einsum(
            "ecd,efd->ecf", scaled_gradient, down_weight_matrix, preferred_element_type=jnp.float32
        )
        + adapter_scale
        * jnp.einsum(
            "uvi,ubi->uvb",
            reduced_gradient,
            adapter_first_factor,
            preferred_element_type=jnp.float32,
        )
    ).astype(jnp.bfloat16)
    adapter_first_gradient = adapter_scale * jnp.einsum(
        "ecf,ecr->efr", hidden, reduced_gradient, preferred_element_type=jnp.float32
    )
    adapter_second_gradient = adapter_scale * jnp.einsum(
        "ecr,ecd->erd", reduced_input, scaled_gradient, preferred_element_type=jnp.float32
    )
    return (
        hidden_input_gradient,
        adapter_first_gradient,
        adapter_second_gradient,
        router_weight_gradient,
    )


def solution(mesh):
    in_specs = (
        P("expert", "groups"),
        P("expert", "groups"),
        P("expert", "groups"),
        P("expert", "groups", None),
        P("expert", None, None),
        P("expert", None, None),
        P("expert", None, None),
    )
    out_specs = (
        P("expert", "groups", None),
        P("expert", "groups", None),
        P("expert", "groups", None),
        P("expert", "groups"),
    )
    return jax.shard_map(shards, mesh=mesh, in_specs=in_specs, out_specs=out_specs, check_vma=False)
```

profile of v0, /device:TPU:0, one launch (start us, length us, event | category | flops | bytes accessed | tf_op | source)
XLA Modules:
  0.0 308.1 jit_solution(12194230819891567349)
XLA Ops:
  0.6 0.7 bitcast_or_fusion
  1.3 0.7 fusion.40
  2.4 7.0 %gather_fusion.2 = f32[1024]{0:T(1024)S(1)} fusion(f32[128,16]{0,1:T(8,128)S(1)} %fusion.38, s32[1024]{0:T(1024)S(1)} %reshape.223), kind=kCustom, calls=%fused_computation.2 | custom fusion | bytes 16384 | tf_op jit(solution)/shard_map/jit(take_along_axis)/gather | solution.py:34
  10.1 7.6 %scatter_custom_fusion = bf16[1152]{0:T(1024)(128)(2,1)S(1)} fusion(s32[1024]{0:T(1024)S(1)} %bitcast.61, bf16[1024]{0:T(1024)(128)(2,1)S(1)} %reshape.233, bf16[]{:T(256)} %constant.10.clone.1), kind=kCustom, calls=%fused_computation.56 | custom fusion | bytes 2306 | tf_op jit(solution)/shard_map/scatter | solution.py:43
  17.7 0.7 all_to_all.30
  18.3 7.4 %all-to-all-start = ((bf16[16,72,1]{1,2,0:T(2,128)(2,1)}), bf16[16,72,1]{1,2,0:T(2,128)(2,1)S(1)}, u32[]{:S(2)}, u32[]{:S(2)}) async-start(bf16[16,72,1]{1,2,0:T(2,128)(2,1)} %all_to_all.30), calls=%async_computation | async-start | bytes 16384 | tf_op jit(solution)/shard_map/all_to_all | solution.py:51
  25.8 4.3 %scatter_custom_fusion.1 = s32[1152]{0:T(1024)S(1)} fusion(s32[1024]{0:T(1024)S(1)} %bitcast.62, s32[1024]{0:T(1024)S(1)} %reshape.241, s32[]{:T(128)} %constant.17.clone.1), kind=kCustom, calls=%fused_computation.52 | custom fusion | bytes 4612 | tf_op jit(solution)/shard_map/scatter | solution.py:38
  30.3 8.0 %gather_fusion = bf16[1152,4096]{1,0:T(8,128)(2,1)} fusion(bf16[129,4096]{1,0:T(8,128)(2,1)S(1)} %concatenate.9, s32[2048]{0:T(1024)S(1)} %pad_clamp_fusion), kind=kCustom, calls=%fused_computation | custom fusion | bytes 18878976 | tf_op jit(solution)/shard_map/gather | solution.py:48
  38.4 6.2 %all-to-all-start.1 = ((bf16[16,72,4096]{2,1,0:T(8,128)(2,1)}), bf16[16,72,4096]{2,1,0:T(8,128)(2,1)}, u32[]{:S(2)}, u32[]{:S(2)}) async-start(bf16[16,72,4096]{2,1,0:T(8,128)(2,1)} %bitcast.59), calls=%async_computation.1 | async-start | bytes 18874368 | tf_op jit(solution)/shard_map/all_to_all | solution.py:50
  44.6 0.6 convolution_convert_fusion.1
  45.6 167.9 %all-to-all-done.1 = bf16[16,72,4096]{2,1,0:T(8,128)(2,1)} async-done(((bf16[16,72,4096]{2,1,0:T(8,128)(2,1)}), bf16[16,72,4096]{2,1,0:T(8,128)(2,1)}, u32[]{:S(2)}, u32[]{:S(2)}) %all-to-all-start.1) | async-done | bytes 9437216 | tf_op jit(solution)/shard_map/all_to_all | solution.py:50
  213.5 6.4 %fusion.23 = bf16[1152,16]{0,1:T(8,128)(2,1)S(1)} fusion(bf16[1,1152,1,1,1,1,4096]{6,1,5,4,3,2,0:T(8,128)(2,1)} %bitcast.18, f32[1152]{0:T(1024)S(1)} %reshape.205, bf16[1,16,4096]{2,1,0:T(8,128)(2,1)S(1)} %copy-done.3), kind=kOutput, calls=%fused_computation.27 | convolution fusion | flops 165169152 | bytes 9609728 | tf_op jit(solution)/shard_map/wzg,wvg->wzv/dot_general | solution.py:85
  220.0 13.5 %fusion.9 = f32[1152,768]{1,0:T(8,128)} fusion(bf16[1,768,4096]{2,1,0:T(8,128)(2,1)} %param.11, bf16[1,1152,1,1,1,1,4096]{6,1,5,4,3,2,0:T(8,128)(2,1)} %bitcast.18, f32[1152]{0:T(1024)S(1)} %reshape.205), kind=kOutput, calls=%fused_computation.18 | convolution fusion | flops 7261913088 | bytes 19272192 | tf_op jit(solution)/shard_map/ecd,efd->ecf/dot_general | solution.py:89
  233.5 6.1 %fusion.14 = f32[1,16,4096]{2,1,0:T(8,128)} fusion(bf16[1152,16]{0,1:T(8,128)(2,1)S(1)} %convolution_convert_fusion.1, bf16[1152,4096]{1,0:T(8,128)(2,1)} %bitcast.12, f32[1152]{0:T(1024)S(1)} %reshape.205), kind=kOutput, calls=%fused_computation.21 | convolution fusion | flops 165216256 | bytes 9740800 | tf_op jit(solution)/shard_map/ecr,ecd->erd/dot_general | solution.py:103
  239.6 12.6 %fusion.1 = f32[1152]{0:T(1024)S(1)} fusion(bf16[16,72,4096]{2,1,0:T(8,128)(2,1)} %all-to-all-done.1, bf16[1,16,4096]{2,1,0:T(8,128)(2,1)S(1)} %multiply_convert_fusion, bf16[1,768,4096]{2,1,0:T(8,128)(2,1)S(1)} %bitcast.65, bf16[1,1152,16]{2,1,0:T(8,128)(2,1)S(1)} %copy.54, bf16[1,1152,768]{2,1,0:T(8,128)(2,1)S(1)} %copy-done.1), kind=kOutput, calls=%fused_computation.8 | convolution fusion | flops 7438801920 | bytes 17670656 | tf_op jit(solution)/shard_map/ecf,efd->ecd/dot_general | solution.py:74
  252.2 0.7 all_to_all.27
  252.8 40.7 %all-to-all-start.2 = ((f32[16,72,1]{1,2,0:T(1,128)}), f32[16,72,1]{1,2,0:T(1,128)S(1)}, u32[]{:S(2)}, u32[]{:S(2)}) async-start(f32[16,72,1]{1,2,0:T(1,128)} %bitcast.17), calls=%async_computation.2 | async-start | bytes 16384 | tf_op jit(solution)/shard_map/all_to_all | solution.py:83
  293.6 3.9 %fusion.22 = bf16[1,1152,768]{2,1,0:T(8,128)(2,1)} fusion(f32[1152,768]{1,0:T(8,128)} %fusion.9, bf16[1152,16]{0,1:T(8,128)(2,1)S(1)} %fusion.23, bf16[1,768,16]{1,2,0:T(8,128)(2,1)S(1)} %copy-done), kind=kOutput, calls=%fused_computation.26 | convolution fusion | flops 30965760 | bytes 5369856 | tf_op jit(solution)/shard_map/uvi,ubi->uvb/dot_general | solution.py:93
  297.4 1.0 fusion.34
  298.4 1.5 all-to-all-done.2
  300.0 0.5 broadcast.100
  300.5 0.7 reduce.10
  301.2 6.2 %gather_fusion.1 = f32[1024]{0:T(1024)S(1)} fusion(f32[1152]{0:T(1024)S(1)} %all_to_all.29, s32[1024]{0:T(1024)S(1)} %broadcast_clamp_fusion), kind=kCustom, calls=%fused_computation.1 | custom fusion | bytes 12288 | tf_op jit(solution)/shard_map/gather | solution.py:84
  307.5 0.7 copy.56
  (41 shorter events, 1.7 us)
Async XLA Ops:
  0.6 43.9 %copy-start = (bf16[1,768,16]{1,2,0:T(8,128)(2,1)S(1)}, bf16[1,768,16]{1,2,0:T(8,128)(2,1)}, u32[]{:S(2)}) copy-start(bf16[1,768,16]{1,2,0:T(8,128)(2,1)} %param.12) | copy-start | bytes 73732
  2.4 7.2 %copy-start.4 = (s32[128,8]{0,1:T(8,128)S(1)}, s32[128,8]{0,1:T(8,128)}, u32[]{:S(2)}) copy-start(s32[128,8]{0,1:T(8,128)} %param.9) | copy-start | bytes 12292
  2.4 7.4 %copy-start.5 = (bf16[128,8]{0,1:T(8,128)(2,1)S(1)}, bf16[128,8]{0,1:T(8,128)(2,1)}, u32[]{:S(2)}) copy-start(bf16[128,8]{0,1:T(8,128)(2,1)} %param.8) | copy-start | bytes 6148
  2.4 27.8 %copy-start.2 = (bf16[128,4096]{1,0:T(8,128)(2,1)S(1)}, bf16[128,4096]{1,0:T(8,128)(2,1)}, u32[]{:S(2)}) copy-start(bf16[128,4096]{1,0:T(8,128)(2,1)} %param.7) | copy-start | bytes 3145732
  18.3 20.0 %all-to-all-start = ((bf16[16,72,1]{1,2,0:T(2,128)(2,1)}), bf16[16,72,1]{1,2,0:T(2,128)(2,1)S(1)}, u32[]{:S(2)}, u32[]{:S(2)}) async-start(bf16[16,72,1]{1,2,0:T(2,128)(2,1)} %all_to_all.30), calls=%async_computation | async-start | bytes 16384 | tf_op jit(solution)/shard_map/all_to_all | solution.py:51
  38.4 6.2 %copy-start.1 = (bf16[1,1152,768]{2,1,0:T(8,128)(2,1)S(1)}, bf16[1,1152,768]{2,1,0:T(8,128)(2,1)}, u32[]{:S(2)}) copy-start(bf16[1,1152,768]{2,1,0:T(8,128)(2,1)} %param.10) | copy-start | bytes 5308420
  38.4 7.1 %copy-start.3 = (bf16[1,16,4096]{2,1,0:T(8,128)(2,1)S(1)}, bf16[1,16,4096]{2,1,0:T(8,128)(2,1)}, u32[]{:S(2)}) copy-start(bf16[1,16,4096]{2,1,0:T(8,128)(2,1)} %param.13) | copy-start | bytes 393220
  38.4 175.2 %all-to-all-start.1 = ((bf16[16,72,4096]{2,1,0:T(8,128)(2,1)}), bf16[16,72,4096]{2,1,0:T(8,128)(2,1)}, u32[]{:S(2)}, u32[]{:S(2)}) async-start(bf16[16,72,4096]{2,1,0:T(8,128)(2,1)} %bitcast.59), calls=%async_computation.1 | async-start | bytes 18874368 | tf_op jit(solution)/shard_map/all_to_all | solution.py:50
  213.5 26.1 %slice-start = ((s8[6291456]{0:T(1024)(128)(4,1)}), s8[4194304]{0:T(1024)(128)(4,1)S(1)}, s32[]{:S(2)}) async-start(s8[6291456]{0:T(1024)(128)(4,1)} %bitcast.64), calls=%async_computation.3 | async-start | bytes 8388608
  220.0 19.6 %slice-start.1 = ((s8[6291456]{0:T(1024)(128)(4,1)}), s8[2097152]{0:T(1024)(128)(4,1)S(1)}, s32[]{:S(2)}) async-start(s8[6291456]{0:T(1024)(128)(4,1)} %bitcast.64), calls=%async_computation.4 | async-start | bytes 4194304
  252.8 47.1 %all-to-all-start.2 = ((f32[16,72,1]{1,2,0:T(1,128)}), f32[16,72,1]{1,2,0:T(1,128)S(1)}, u32[]{:S(2)}, u32[]{:S(2)}) async-start(f32[16,72,1]{1,2,0:T(1,128)} %bitcast.17), calls=%async_computation.2 | async-start | bytes 16384 | tf_op jit(solution)/shard_map/all_to_all | solution.py:83
where the time goes:
time: 309 us; the launch traced here: 308 us
  waiting for transfers between devices  169 us (55%)
  starting transfers between devices  54.3 us (18%)
  matrix products  44.2 us (14%)
  local copies, waits for them, and re-layouts  37.1 us (12%)
    all_to_all x1, waiting for transfers between devices, shards(): lax.all_to_all(send_rows, 'expert', split_axis=0, concat_axis=0, tiled=True)  168 us
    all_to_all x1, starting transfers between devices, shards(): lax.all_to_all(send_back, 'expert', split_axis=0, concat_axis=0, tiled=True)  40.7 us
    dot_general x1, matrix products, shards(): jnp.einsum('ecd,efd->ecf', scaled_gradient, down_weight_matrix, preferred...  13.5 us
    dot_general x1, matrix products, shards(): jnp.einsum('ecf,efd->ecd', joined_input, joined_weight, preferred_element...  12.6 us
    gather x1, local copies, waits for them, and re-layouts, shards(): send_rows = padded[slot_token_index]  8.02 us
    scatter x1, local copies, waits for them, and re-layouts, shards(): slot_router_weight = jnp.zeros((expert_count * per_source,), jnp.bfloat16...  7.59 us
    all_to_all x1, starting transfers between devices, shards(): lax.all_to_all(slot_router_weight, 'expert', split_axis=0, concat_axis=0,...  7.39 us
    gather x5, local copies, waits for them, and re-layouts, shards(): position = jnp.take_along_axis(before, routes, axis=1).astype(jnp.int32)  7.36 us
  transfers between devices with their start and end apart: 3, of which 2 were waited for; matrix products, arithmetic and copies ran while one was open for 6% of the time, Pallas kernels for 0%

commit v1 on v0

--- a/solution.py
+++ b/solution.py
@@ -1,9 +1,399 @@
+import functools
+
 import jax
 import jax.numpy as jnp
 from jax import lax
+from jax.experimental import pallas as pl
+from jax.experimental.pallas import tpu as pltpu
 from jax.sharding import PartitionSpec as P
 
 adapter_scale = 2.0
+MIB = 1 << 20
+
+
+def dot(a, b, dims):
+    return lax.dot_general(a, b, ((dims[:1], dims[1:]), ((), ())), preferred_element_type=jnp.float32)
+
+
+def ring_kernel(
+    peers,
+    per_source,
+    strip,
+    grad_hbm,
+    weight_ref,
+    routes_ref,
+    hidden_ref,
+    down_hbm,
+    first_ref,
+    second_ref,
+    out_ref,
+    first_out,
+    second_out,
+    router_out,
+    gathered,
+    down,
+    low_in,
+    wide,
+    thin,
+    meta_out,
+    meta_in,
+    router_send,
+    router_recv,
+    right_send,
+    right_recv,
+    left_send,
+    left_recv,
+    pair_send,
+    pair_recv,
+    meta_send,
+    meta_got,
+    back_send,
+    back_got,
+    local_sem,
+):
+    tokens, width = grad_hbm.shape
+    inner = hidden_ref.shape[1]
+    top = routes_ref.shape[1]
+    half = tokens // 2
+    chips = peers // 2
+    side = chips // 2
+    slots = 2 * per_source
+    far = chips // 2
+    last = 2 * (far - 1)
+
+    me = lax.axis_index("expert")
+    core = lax.rem(me, 2)
+    chip = lax.div(me, 2)
+    row, column = lax.div(chip, 2), lax.rem(chip, 2)
+    place = row + column * (chips - 1 - 2 * row)
+
+    def chip_at(position):
+        position = lax.rem(position + chips, chips)
+        col = lax.div(position, side)
+        return 2 * (position + col * (chips - 1 - 2 * position)) + col
+
+    def device(index):
+        return dict(device_id={"expert": index}, device_id_type=pl.DeviceIdType.MESH)
+
+    right = 2 * chip_at(place + 1) + core
+    left = 2 * chip_at(place - 1) + core
+    sibling = chip * 2 + 1 - core
+
+    barrier = pltpu.get_barrier_semaphore()
+    for ahead in range(1, peers):
+        pl.semaphore_signal(barrier, inc=1, **device(lax.rem(me + ahead, peers)))
+
+    down_copy = pltpu.make_async_copy(down_hbm, down, local_sem.at[0])
+    down_copy.start()
+    own_copy = pltpu.make_async_copy(grad_hbm, gathered.at[chip, core], local_sem.at[1])
+    own_copy.start()
+
+    expert_at = lax.broadcasted_iota(jnp.int32, (tokens, peers), 1)
+    member = jnp.zeros((tokens, peers), jnp.float32)
+    table = jnp.zeros((tokens, peers), jnp.float32)
+    for k in range(top):
+        same = routes_ref[:, k : k + 1] == expert_at
+        member += jnp.where(same, 1.0, 0.0)
+        table += jnp.where(same, weight_ref[:, k : k + 1].astype(jnp.float32), 0.0)
+    at0 = lax.broadcasted_iota(jnp.int32, (tokens, tokens), 0)
+    at1 = lax.broadcasted_iota(jnp.int32, (tokens, tokens), 1)
+    earlier = jnp.where(at0 < at1, 1.0, 0.0).astype(jnp.bfloat16)
+    unit = jnp.where(at0 == at1, 1.0, 0.0).astype(jnp.bfloat16)
+    member = member.astype(jnp.bfloat16)
+    before = dot(member, earlier, (0, 0))
+    position = jnp.where(dot(member, unit, (0, 0)) > 0.5, before, -1.0)
+    weights = dot(table.astype(jnp.bfloat16), unit, (0, 0))
+    meta_out[...] = jnp.zeros_like(meta_out)
+    for e in range(peers):
+        meta_out[e, 0:1, :] = position[e : e + 1, :]
+        meta_out[e, 1:2, :] = weights[e : e + 1, :]
+
+    pl.semaphore_wait(barrier, peers - 1)
+
+    def rows(chunk):
+        return pl.ds(chunk * half, half)
+
+    def send_right(k):
+        step, chunk = k // 2, k % 2
+        target = gathered.at[chip_at(place - step), core, rows(chunk)]
+        return pltpu.make_async_remote_copy(
+            src_ref=grad_hbm.at[rows(chunk)] if step == 0 else target,
+            dst_ref=target,
+            send_sem=right_send.at[k],
+            recv_sem=right_recv.at[k],
+            **device(right),
+        )
+
+    def send_left(k):
+        step, chunk = k // 2, 1 - k % 2
+        target = gathered.at[chip_at(place + step), core, rows(chunk)]
+        return pltpu.make_async_remote_copy(
+            src_ref=grad_hbm.at[rows(chunk)] if step == 0 else target,
+            dst_ref=target,
+            send_sem=left_send.at[k],
+            recv_sem=left_recv.at[k],
+            **device(left),
+        )
+
+    def from_left(k):
+        block = gathered.at[chip_at(place - 1 - k // 2), core, rows(k % 2)]
+        return pltpu.make_async_remote_copy(
+            src_ref=block, dst_ref=block, send_sem=right_send.at[k], recv_sem=right_recv.at[k],
+            **device(left),
+        )
+
+    def from_right(k):
+        block = gathered.at[chip_at(place + 1 + k // 2), core, rows(1 - k % 2)]
+        return pltpu.make_async_remote_copy(
+            src_ref=block, dst_ref=block, send_sem=left_send.at[k], recv_sem=left_recv.at[k],
+            **device(right),
+        )
+
+    def pair_copy(number, block, source=None):
+        return pltpu.make_async_remote_copy(
+            src_ref=block if source is None else source,
+            dst_ref=block,
+            send_sem=pair_send.at[number],
+            recv_sem=pair_recv.at[number],
+            **device(sibling),
+        )
+
+    def pair_left(k, at_core):
+        return pair_copy(1 + k, gathered.at[chip_at(place - 1 - k // 2), at_core, rows(k % 2)])
+
+    def pair_right(k, at_core):
+        block = gathered.at[chip_at(place + 1 + k // 2), at_core, rows(1 - k % 2)]
+        return pair_copy(2 + last + k, block)
+
+    for k in range(2):
+        send_right(k).start()
+        send_left(k).start()
+    own_pair = pair_copy(0, gathered.at[chip, core], grad_hbm)
+    own_pair.start()
+
+    def meta_copy(target):
+        return pltpu.make_async_remote_copy(
+            src_ref=meta_out.at[target],
+            dst_ref=meta_in.at[me],
+            send_sem=meta_send.at[target],
+            recv_sem=meta_got.at[me],
+            **device(target),
+        )
+
+    def send_meta(ahead, carry):
+        meta_copy(lax.rem(me + ahead, peers)).start()
+        return carry
+
+    lax.fori_loop(1, peers, send_meta, 0)
+    meta_in[me] = meta_out[me]
+
+    first_out[...] = jnp.zeros_like(first_out)
+    second_out[...] = jnp.zeros_like(second_out)
+    low_in[...] = dot(hidden_ref[...], first_ref[...], (1, 0)).astype(jnp.bfloat16)
+
+    def wait_meta(ahead, carry):
+        source = lax.rem(me + ahead, peers)
+        pltpu.make_async_remote_copy(
+            src_ref=meta_out.at[source],
+            dst_ref=meta_in.at[source],
+            send_sem=meta_send.at[source],
+            recv_sem=meta_got.at[source],
+            **device(source),
+        ).wait()
+        return carry
+
+    lax.fori_loop(1, peers, wait_meta, 0)
+    down_copy.wait()
+    own_copy.wait()
+
+    def back_copy(target):
+        return pltpu.make_async_remote_copy(
+            src_ref=router_send.at[target],
+            dst_ref=router_recv.at[me],
+            send_sem=back_send.at[target],
+            recv_sem=back_got.at[me],
+            **device(target),
+        )
+
+    def work(which):
+        where = pl.ds(pl.multiple_of(which * slots, 16), slots)
+        meta0, meta1 = meta_in[2 * which], meta_in[2 * which + 1]
+        high = meta1[0:1, :]
+        high = jnp.where(high < 0.0, -1.0, high + float(per_source))
+        slot_of = jnp.concatenate([meta0[0:1, :], high], axis=1)
+        weight = jnp.concatenate([meta0[1:2, :], meta1[1:2, :]], axis=1)
+        slot_at = lax.broadcasted_iota(jnp.int32, (slots, 2 * tokens), 0).astype(jnp.float32)
+        pick = jnp.where(slot_at == slot_of, 1.0, 0.0)
+        slot_weight = jnp.sum(pick * weight, axis=1, keepdims=True)
+        pick16 = pick.astype(jnp.bfloat16)
+        hidden = hidden_ref[where, :]
+        weighted = (slot_weight * low_in[where, :].astype(jnp.float32)).astype(jnp.bfloat16)
+        mixed = dot(weighted, pick16, (0, 0)).astype(jnp.bfloat16)
+        both = jnp.concatenate([pick16, mixed], axis=0)
+        wide[...] = jnp.zeros_like(wide)
+        thin[...] = jnp.zeros_like(thin)
+
+        def strip_step(at, carry):
+            lanes = pl.ds(pl.multiple_of(at * strip, strip), strip)
+            block = gathered[which, :, :, lanes].reshape(2 * tokens, strip)
+            product = dot(both, block, (1, 0))
+            slot_rows = product[:slots].astype(jnp.bfloat16)
+            second_out[:, lanes] += adapter_scale * product[slots:]
+            wide[...] += dot(slot_rows, down[:, lanes], (1, 1))
+            thin[...] += dot(slot_rows, second_ref[:, lanes], (1, 1))
+            return carry
+
+        lax.fori_loop(0, width // strip, strip_step, 0)
+        low = thin[...]
+        total = wide[...] + adapter_scale * dot(low.astype(jnp.bfloat16), first_ref[...], (1, 1))
+        out_ref[where, :] = (slot_weight * total).astype(jnp.bfloat16)
+        low_grad = (slot_weight * low).astype(jnp.bfloat16)
+        first_out[...] += adapter_scale * dot(low_grad, hidden, (0, 0))
+        router = jnp.sum(hidden.astype(jnp.float32) * total, axis=1, keepdims=True)
+        routed = jnp.sum(pick * router, axis=0, keepdims=True)
+        router_send[2 * which] = jnp.broadcast_to(routed[:, :tokens], (8, tokens))
+        router_send[2 * which + 1] = jnp.broadcast_to(routed[:, tokens:], (8, tokens))
+
+    def work_and_return(which):
+        work(which)
+        back_copy(2 * which).start()
+        back_copy(2 * which + 1).start()
+
+    for k in range(last + 1):
+        from_left(k).wait_recv()
+        if k + 2 <= last:
+            send_right(k + 2).start()
+        pair_left(k, core).start()
+        from_right(k).wait_recv()
+        if k + 2 <= last:
+            send_left(k + 2).start()
+        pair_right(k, core).start()
+        if k == 0:
+            pair_copy(0, gathered.at[chip, 1 - core]).wait_recv()
+            work(chip)
+            back_copy(sibling).start()
+            router_recv[me] = router_send[me]
+        elif k == last:
+            pair_left(k, 1 - core).wait_recv()
+            pair_right(k, 1 - core).wait_recv()
+            work_and_return(chip_at(place + far))
+        else:
+            step = (k - 1) // 2
+            if k % 2 == 1:
+                for j in (2 * step, 2 * step + 1):
+                    pair_left(j, 1 - core).wait_recv()
+                work_and_return(chip_at(place - 1 - step))
+            if k % 2 == 0 or k + 1 == last:
+                for j in (2 * step, 2 * step + 1):
+                    pair_right(j, 1 - core).wait_recv()
+                work_and_return(chip_at(place + 1 + step))
+
+    for k in range(last + 1):
+        send_right(k).wait_send()
+        send_left(k).wait_send()
+        pair_left(k, core).wait_send()
+        pair_right(k, core).wait_send()
+    own_pair.wait_send()
+
+    def wait_back(ahead, carry):
+        source = lax.rem(me + ahead, peers)
+        pltpu.make_async_remote_copy(
+            src_ref=router_send.at[source],
+            dst_ref=router_recv.at[source],
+            send_sem=back_send.at[source],
+            recv_sem=back_got.at[source],
+            **device(source),
+        ).wait()
+        return carry
+
+    lax.fori_loop(1, peers, wait_back, 0)
+    router_out[...] = router_recv[...]
+
+
+def ring_shards(
+    output_gradient,
+    router_weight_table,
+    routes,
+    hidden,
+    down_weight_matrix,
+    adapter_first_factor,
+    adapter_second_factor,
+):
+    peers = lax.axis_size("expert")
+    tokens, width = output_gradient.shape
+    _, capacity, inner = hidden.shape
+    rank = adapter_first_factor.shape[2]
+    per_source = capacity // peers
+    chips = peers // 2
+    steps = 2 * (chips // 2 - 1) + 1
+    strip = 1024 if width % 1024 == 0 else 128
+    vmem = pl.BlockSpec(memory_space=pltpu.VMEM)
+    hbm = pl.BlockSpec(memory_space=pl.ANY)
+    dma = pltpu.SemaphoreType.DMA
+    small = (peers, 8, tokens)
+    grad, first, second, router = pl.pallas_call(
+        functools.partial(ring_kernel, peers, per_source, strip),
+        out_shape=(
+            jax.ShapeDtypeStruct((capacity, inner), jnp.bfloat16),
+            jax.ShapeDtypeStruct((rank, inner), jnp.float32),
+            jax.ShapeDtypeStruct((rank, width), jnp.float32),
+            jax.ShapeDtypeStruct(small, jnp.float32),
+        ),
+        in_specs=[hbm, vmem, vmem, vmem, hbm, vmem, vmem],
+        out_specs=(vmem, vmem, vmem, vmem),
+        scratch_shapes=[
+            pltpu.VMEM((chips, 2, tokens, width), jnp.bfloat16),
+            pltpu.VMEM((inner, width), jnp.bfloat16),
+            pltpu.VMEM((capacity, rank), jnp.bfloat16),
+            pltpu.VMEM((2 * per_source, inner), jnp.float32),
+            pltpu.VMEM((2 * per_source, rank), jnp.float32),
+            pltpu.VMEM(small, jnp.float32),
+            pltpu.VMEM(small, jnp.float32),
+            pltpu.VMEM(small, jnp.float32),
+            pltpu.VMEM(small, jnp.float32),
+            dma((steps,)),
+            dma((steps,)),
+            dma((steps,)),
+            dma((steps,)),
+            dma((2 * steps + 1,)),
+            dma((2 * steps + 1,)),
+            dma((peers,)),
+            dma((peers,)),
+            dma((peers,)),
+            dma((peers,)),
+            dma((2,)),
+        ],
+        compiler_params=pltpu.CompilerParams(
+            collective_id=0, has_side_effects=True, vmem_limit_bytes=56 * MIB
+        ),
+    )(
+        output_gradient,
+        router_weight_table,
+        routes,
+        hidden[0],
+        down_weight_matrix[0],
+        adapter_first_factor[0],
+        adapter_second_factor[0],
+    )
+    by_expert = router[:, 0, :].T
+    chosen = routes[:, :, None] == jnp.arange(peers, dtype=jnp.int32)
+    router_weight_gradient = jnp.sum(jnp.where(chosen, by_expert[:, None, :], 0.0), axis=2)
+    return grad[None], first.T[None], second[None], router_weight_gradient
+
+
+def ring_fits(peers, tokens_dev, width, experts, capacity, inner):
+    per_source = capacity // peers
+    gathered = peers * tokens_dev * width * 2
+    return (
+        experts == peers
+        and peers >= 8
+        and peers % 4 == 0
+        and tokens_dev == 128
+        and width % 128 == 0
+        and inner % 128 == 0
+        and (2 * per_source) % 16 == 0
+        and gathered + inner * width * 2 + 3 * capacity * inner * 2 <= 40 * MIB
+    )
 
 
 def shards(
@@ -127,4 +517,22 @@
         P("expert", "groups", None),
         P("expert", "groups"),
     )
-    return jax.shard_map(shards, mesh=mesh, in_specs=in_specs, out_specs=out_specs, check_vma=False)
+
+    def call(*arrays):
+        peers = mesh.shape["expert"]
+        groups = mesh.shape["groups"]
+        gradient, hidden = arrays[0], arrays[3]
+        fits = ring_fits(
+            peers,
+            gradient.shape[0] // peers,
+            gradient.shape[1] // groups,
+            hidden.shape[0],
+            hidden.shape[1] // groups,
+            hidden.shape[2],
+        )
+        body = ring_shards if fits else shards
+        return jax.shard_map(
+            body, mesh=mesh, in_specs=in_specs, out_specs=out_specs, check_vma=False
+        )(*arrays)
+
+    return call

time: 309 us -> 116 us (0.38)
  waiting for transfers between devices: 169 us -> 0 us
  Pallas kernels: 0 us -> 105 us
  starting transfers between devices: 54.3 us -> 0 us
  matrix products: 44.2 us -> 0 us
  local copies, waits for them, and re-layouts: 37.1 us -> 9.38 us
    all_to_all x3 -> x0, waiting for transfers between devices: 169 us -> none  [the longest x1 168 us: shards(): lax.all_to_all(send_rows, 'expert', split_axis=0, concat_axis=0, tiled=True)]
    pallas_call x0 -> x1, Pallas kernels: none -> 105 us  [ring_shards(): pl.pallas_call(functools.partial(ring_kernel, peers, per_source, strip),...]
    all_to_all x3 -> x0, starting transfers between devices: 54.3 us -> none  [the longest x1 40.7 us: shards(): lax.all_to_all(send_back, 'expert', split_axis=0, concat_axis=0, tiled=True)]
    dot_general x8 -> x0, matrix products: 44.2 us -> none  [the longest x1 13.5 us: shards(): jnp.einsum('ecd,efd->ecf', scaled_gradient, down_weight_matrix, preferred...]
    gather x7 -> x0, local copies, waits for them, and re-layouts: 21.5 us -> none  [the longest x1 8.02 us: shards(): send_rows = padded[slot_token_index]]
    scatter x2 -> x0, local copies, waits for them, and re-layouts: 11.9 us -> none  [the longest x1 7.59 us: shards(): slot_router_weight = jnp.zeros((expert_count * per_source,), jnp.bfloat16...]
    unnamed x18 -> x12, local copies, waits for them, and re-layouts: 0.82 us -> 8.54 us
  transfers between devices with their start and end apart: 3 -> 0, of which waited for: 2 -> 0; matrix products, arithmetic and copies ran while one was open for 6% -> 0% of each run, Pallas kernels for 0% -> 0%
where the time goes in v1:
time: 116 us
  Pallas kernels  105 us (91%)
  local copies, waits for them, and re-layouts  9.38 us (8%)
    pallas_call x1, Pallas kernels, ring_shards(): pl.pallas_call(functools.partial(ring_kernel, peers, per_source, strip),...  105 us
    unnamed x12, local copies, waits for them, and re-layouts  8.54 us

profile of v1, /device:TPU:0, one launch (start us, length us, event | category | flops | bytes accessed | tf_op | source)
XLA Modules:
  0.0 115.8 jit_solution(2858554370728982475)
XLA Ops:
  0.6 1.4 %copy.17.weight_ref = bf16[128,8]{1,0:T(8,128)(2,1)} copy(bf16[128,8]{0,1:T(8,128)(2,1)} %param.8) | data formatting | bytes 4096 | tf_op args[1]
  2.0 1.4 %copy.18.routes_ref = s32[128,8]{1,0:T(8,128)} copy(s32[128,8]{0,1:T(8,128)} %param.9) | data formatting | bytes 8192 | tf_op args[2]
  3.4 1.6 %copy.16 = bf16[1,768,16]{2,1,0:T(8,128)(2,1)} copy(bf16[1,768,16]{1,2,0:T(8,128)(2,1)} %param.12) | data formatting | bytes 49152 | tf_op args[5]
  5.0 0.0 copy-start.2
  5.0 105.2 %shard_map.102 = (bf16[1152,768]{1,0:T(8,128)(2,1)}, f32[16,768]{1,0:T(8,128)}, f32[16,4096]{1,0:T(8,128)}, f32[16,8,128]{2,1,0:T(8,128)}) custom-call(bf16[128,4096]{1,0:T(8,128)(2,1)} %grad_hbm.1, bf16[128,8]{1,0:T(8,128)(2,1)} %copy.17.weight_ref, s32[128,8]{1,0:T(8,128)} %copy.18.routes_ref, bf16[1152,768]{1,0:T(8,128)(2,1)} %bitcast.13, ...), custom_call_target="tpu_custom_call" | custom-call | tf_op jit(solution)/shard_map/pallas_call | solution.py:334
  110.2 0.8 slice.3
  111.1 0.0 copy-done.2
  111.1 0.6 select_reduce_fusion
  111.7 0.0 copy-start.1
  111.7 0.0 copy-start
  111.7 2.8 %copy.22 = bf16[1,1152,768]{2,1,0:T(8,128)(2,1)} copy(bf16[1,1152,768]{2,1,0:T(8,128)(2,1)} %bitcast.14) | data formatting | bytes 3538944
  114.5 0.0 copy-done.1
  114.5 0.6 copy.23
  115.1 0.0 copy-done
  115.1 0.7 copy.24
Async XLA Ops:
  5.0 106.1 %copy-start.2 = (s32[128,8]{0,1:T(8,128)S(1)}, s32[128,8]{0,1:T(8,128)}, u32[]{:S(2)}) copy-start(s32[128,8]{0,1:T(8,128)} %param.9) | copy-start | bytes 12292
  111.7 2.8 %copy-start.1 = (f32[16,768]{1,0:T(8,128)S(1)}, f32[16,768]{1,0:T(8,128)}, u32[]{:S(2)}) copy-start(f32[16,768]{1,0:T(8,128)} %get-tuple-element.9) | copy-start | bytes 147460
  111.7 3.5 %copy-start = (f32[16,4096]{1,0:T(8,128)S(1)}, f32[16,4096]{1,0:T(8,128)}, u32[]{:S(2)}) copy-start(f32[16,4096]{1,0:T(8,128)} %get-tuple-element.10) | copy-start | bytes 786436

commit v2 on v1

--- a/solution.py
+++ b/solution.py
@@ -19,19 +19,22 @@
     peers,
     per_source,
     strip,
+    parts,
     grad_hbm,
     weight_ref,
     routes_ref,
-    hidden_ref,
+    hidden_hbm,
     down_hbm,
     first_ref,
     second_ref,
-    out_ref,
+    out_hbm,
     first_out,
     second_out,
     router_out,
     gathered,
     down,
+    hidden_ref,
+    out_ref,
     low_in,
     wide,
     thin,
@@ -50,16 +53,17 @@
     back_send,
     back_got,
     local_sem,
+    out_sem,
 ):
     tokens, width = grad_hbm.shape
     inner = hidden_ref.shape[1]
-    top = routes_ref.shape[1]
-    half = tokens // 2
+    top = routes_ref.shape[0]
+    piece = width // parts
     chips = peers // 2
     side = chips // 2
     slots = 2 * per_source
     far = chips // 2
-    last = 2 * (far - 1)
+    last = parts * (far - 1) + parts // 2 - 1
 
     me = lax.axis_index("expert")
     core = lax.rem(me, 2)
@@ -87,22 +91,21 @@
     down_copy.start()
     own_copy = pltpu.make_async_copy(grad_hbm, gathered.at[chip, core], local_sem.at[1])
     own_copy.start()
-
-    expert_at = lax.broadcasted_iota(jnp.int32, (tokens, peers), 1)
-    member = jnp.zeros((tokens, peers), jnp.float32)
-    table = jnp.zeros((tokens, peers), jnp.float32)
+    hidden_copy = pltpu.make_async_copy(hidden_hbm, hidden_ref, local_sem.at[2])
+    hidden_copy.start()
+
+    expert_at = lax.broadcasted_iota(jnp.int32, (peers, tokens), 0)
+    member = jnp.zeros((peers, tokens), jnp.float32)
+    weights = jnp.zeros((peers, tokens), jnp.float32)
     for k in range(top):
-        same = routes_ref[:, k : k + 1] == expert_at
+        same = routes_ref[k : k + 1, :] == expert_at
         member += jnp.where(same, 1.0, 0.0)
-        table += jnp.where(same, weight_ref[:, k : k + 1].astype(jnp.float32), 0.0)
+        weights += jnp.where(same, weight_ref[k : k + 1, :].astype(jnp.float32), 0.0)
     at0 = lax.broadcasted_iota(jnp.int32, (tokens, tokens), 0)
     at1 = lax.broadcasted_iota(jnp.int32, (tokens, tokens), 1)
     earlier = jnp.where(at0 < at1, 1.0, 0.0).astype(jnp.bfloat16)
-    unit = jnp.where(at0 == at1, 1.0, 0.0).astype(jnp.bfloat16)
-    member = member.astype(jnp.bfloat16)
-    before = dot(member, earlier, (0, 0))
-    position = jnp.where(dot(member, unit, (0, 0)) > 0.5, before, -1.0)
-    weights = dot(table.astype(jnp.bfloat16), unit, (0, 0))
+    before = dot(member.astype(jnp.bfloat16), earlier, (1, 0))
+    position = jnp.where(member > 0.5, before, -1.0)
     meta_out[...] = jnp.zeros_like(meta_out)
     for e in range(peers):
         meta_out[e, 0:1, :] = position[e : e + 1, :]
@@ -110,14 +113,14 @@
 
     pl.semaphore_wait(barrier, peers - 1)
 
-    def rows(chunk):
-        return pl.ds(chunk * half, half)
+    def lanes_of(chunk):
+        return pl.ds(chunk * piece, piece)
 
     def send_right(k):
-        step, chunk = k // 2, k % 2
-        target = gathered.at[chip_at(place - step), core, rows(chunk)]
-        return pltpu.make_async_remote_copy(
-            src_ref=grad_hbm.at[rows(chunk)] if step == 0 else target,
+        step, chunk = k // parts, k % parts
+        target = gathered.at[chip_at(place - step), core, :, lanes_of(chunk)]
+        return pltpu.make_async_remote_copy(
+            src_ref=grad_hbm.at[:, lanes_of(chunk)] if step == 0 else target,
             dst_ref=target,
             send_sem=right_send.at[k],
             recv_sem=right_recv.at[k],
@@ -125,10 +128,10 @@
         )
 
     def send_left(k):
-        step, chunk = k // 2, 1 - k % 2
-        target = gathered.at[chip_at(place + step), core, rows(chunk)]
-        return pltpu.make_async_remote_copy(
-            src_ref=grad_hbm.at[rows(chunk)] if step == 0 else target,
+        step, chunk = k // parts, parts - 1 - k % parts
+        target = gathered.at[chip_at(place + step), core, :, lanes_of(chunk)]
+        return pltpu.make_async_remote_copy(
+            src_ref=grad_hbm.at[:, lanes_of(chunk)] if step == 0 else target,
             dst_ref=target,
             send_sem=left_send.at[k],
             recv_sem=left_recv.at[k],
@@ -136,14 +139,14 @@
         )
 
     def from_left(k):
-        block = gathered.at[chip_at(place - 1 - k // 2), core, rows(k % 2)]
+        block = gathered.at[chip_at(place - 1 - k // parts), core, :, lanes_of(k % parts)]
         return pltpu.make_async_remote_copy(
             src_ref=block, dst_ref=block, send_sem=right_send.at[k], recv_sem=right_recv.at[k],
             **device(left),
         )
 
     def from_right(k):
-        block = gathered.at[chip_at(place + 1 + k // 2), core, rows(1 - k % 2)]
+        block = gathered.at[chip_at(place + 1 + k // parts), core, :, lanes_of(parts - 1 - k % parts)]
         return pltpu.make_async_remote_copy(
             src_ref=block, dst_ref=block, send_sem=left_send.at[k], recv_sem=left_recv.at[k],
             **device(right),
@@ -159,13 +162,14 @@
         )
 
     def pair_left(k, at_core):
-        return pair_copy(1 + k, gathered.at[chip_at(place - 1 - k // 2), at_core, rows(k % 2)])
+        block = gathered.at[chip_at(place - 1 - k // parts), at_core, :, lanes_of(k % parts)]
+        return pair_copy(1 + k, block)
 
     def pair_right(k, at_core):
-        block = gathered.at[chip_at(place + 1 + k // 2), at_core, rows(1 - k % 2)]
+        block = gathered.at[chip_at(place + 1 + k // parts), at_core, :, lanes_of(parts - 1 - k % parts)]
         return pair_copy(2 + last + k, block)
 
-    for k in range(2):
+    for k in range(parts):
         send_right(k).start()
         send_left(k).start()
     own_pair = pair_copy(0, gathered.at[chip, core], grad_hbm)
@@ -189,7 +193,8 @@
 
     first_out[...] = jnp.zeros_like(first_out)
     second_out[...] = jnp.zeros_like(second_out)
-    low_in[...] = dot(hidden_ref[...], first_ref[...], (1, 0)).astype(jnp.bfloat16)
+    hidden_copy.wait()
+    low_in[...] = dot(hidden_ref[...], first_ref[...], (1, 1)).astype(jnp.bfloat16)
 
     def wait_meta(ahead, carry):
         source = lax.rem(me + ahead, peers)
@@ -214,6 +219,10 @@
             recv_sem=back_got.at[me],
             **device(target),
         )
+
+    def out_copy(which):
+        where = pl.ds(pl.multiple_of(which * slots, 16), slots)
+        return pltpu.make_async_copy(out_ref.at[where, :], out_hbm.at[where, :], out_sem.at[which])
 
     def work(which):
         where = pl.ds(pl.multiple_of(which * slots, 16), slots)
@@ -245,8 +254,9 @@
 
         lax.fori_loop(0, width // strip, strip_step, 0)
         low = thin[...]
-        total = wide[...] + adapter_scale * dot(low.astype(jnp.bfloat16), first_ref[...], (1, 1))
+        total = wide[...] + adapter_scale * dot(low.astype(jnp.bfloat16), first_ref[...], (1, 0))
         out_ref[where, :] = (slot_weight * total).astype(jnp.bfloat16)
+        out_copy(which).start()
         low_grad = (slot_weight * low).astype(jnp.bfloat16)
         first_out[...] += adapter_scale * dot(low_grad, hidden, (0, 0))
         router = jnp.sum(hidden.astype(jnp.float32) * total, axis=1, keepdims=True)
@@ -259,34 +269,41 @@
         back_copy(2 * which).start()
         back_copy(2 * which + 1).start()
 
+    def wait_left(step, count):
+        for k in range(parts * step, parts * step + count):
+            pair_left(k, 1 - core).wait_recv()
+
+    def wait_right(step, count):
+        for k in range(parts * step, parts * step + count):
+            pair_right(k, 1 - core).wait_recv()
+
     for k in range(last + 1):
         from_left(k).wait_recv()
-        if k + 2 <= last:
-            send_right(k + 2).start()
+        if k + parts <= last:
+            send_right(k + parts).start()
         pair_left(k, core).start()
         from_right(k).wait_recv()
-        if k + 2 <= last:
-            send_left(k + 2).start()
+        if k + parts <= last:
+            send_left(k + parts).start()
         pair_right(k, core).start()
         if k == 0:
             pair_copy(0, gathered.at[chip, 1 - core]).wait_recv()
             work(chip)
             back_copy(sibling).start()
             router_recv[me] = router_send[me]
-        elif k == last:
-            pair_left(k, 1 - core).wait_recv()
-            pair_right(k, 1 - core).wait_recv()
+        step = (k + 1) // parts - 1
+        if k % parts == parts - 1:
+            wait_left(step, parts)
+            work_and_return(chip_at(place - 1 - step))
+        if (k % parts == 0 and k > 0 and k < last) or (k + 1 == last and k % parts == parts - 1):
+            if k % parts == 0:
+                step = k // parts - 1
+            wait_right(step, parts)
+            work_and_return(chip_at(place + 1 + step))
+        if k == last:
+            wait_left(far - 1, parts // 2)
+            wait_right(far - 1, parts // 2)
             work_and_return(chip_at(place + far))
-        else:
-            step = (k - 1) // 2
-            if k % 2 == 1:
-                for j in (2 * step, 2 * step + 1):
-                    pair_left(j, 1 - core).wait_recv()
-                work_and_return(chip_at(place - 1 - step))
-            if k % 2 == 0 or k + 1 == last:
-                for j in (2 * step, 2 * step + 1):
-                    pair_right(j, 1 - core).wait_recv()
-                work_and_return(chip_at(place + 1 + step))
 
     for k in range(last + 1):
         send_right(k).wait_send()
@@ -307,7 +324,12 @@
         return carry
 
     lax.fori_loop(1, peers, wait_back, 0)
-    router_out[...] = router_recv[...]
+    returned = router_recv[:, 0, :]
+    for k in range(top):
+        same = routes_ref[k : k + 1, :] == expert_at
+        router_out[k : k + 1, :] = jnp.sum(jnp.where(same, returned, 0.0), axis=0, keepdims=True)
+    for which in range(chips):
+        out_copy(which).wait()
 
 
 def ring_shards(
@@ -325,25 +347,29 @@
     rank = adapter_first_factor.shape[2]
     per_source = capacity // peers
     chips = peers // 2
-    steps = 2 * (chips // 2 - 1) + 1
-    strip = 1024 if width % 1024 == 0 else 128
+    parts = 4
+    steps = parts * (chips // 2 - 1) + parts // 2
+    top = routes.shape[1]
+    strip = 1024
     vmem = pl.BlockSpec(memory_space=pltpu.VMEM)
     hbm = pl.BlockSpec(memory_space=pl.ANY)
     dma = pltpu.SemaphoreType.DMA
     small = (peers, 8, tokens)
     grad, first, second, router = pl.pallas_call(
-        functools.partial(ring_kernel, peers, per_source, strip),
+        functools.partial(ring_kernel, peers, per_source, strip, parts),
         out_shape=(
             jax.ShapeDtypeStruct((capacity, inner), jnp.bfloat16),
             jax.ShapeDtypeStruct((rank, inner), jnp.float32),
             jax.ShapeDtypeStruct((rank, width), jnp.float32),
-            jax.ShapeDtypeStruct(small, jnp.float32),
+            jax.ShapeDtypeStruct((top, tokens), jnp.float32),
         ),
-        in_specs=[hbm, vmem, vmem, vmem, hbm, vmem, vmem],
-        out_specs=(vmem, vmem, vmem, vmem),
+        in_specs=[hbm, vmem, vmem, hbm, hbm, vmem, vmem],
+        out_specs=(hbm, vmem, vmem, vmem),
         scratch_shapes=[
             pltpu.VMEM((chips, 2, tokens, width), jnp.bfloat16),
             pltpu.VMEM((inner, width), jnp.bfloat16),
+            pltpu.VMEM((capacity, inner), jnp.bfloat16),
+            pltpu.VMEM((capacity, inner), jnp.bfloat16),
             pltpu.VMEM((capacity, rank), jnp.bfloat16),
             pltpu.VMEM((2 * per_source, inner), jnp.float32),
             pltpu.VMEM((2 * per_source, rank), jnp.float32),
@@ -361,24 +387,22 @@
             dma((peers,)),
             dma((peers,)),
             dma((peers,)),
-            dma((2,)),
+            dma((3,)),
+            dma((chips,)),
         ],
         compiler_params=pltpu.CompilerParams(
             collective_id=0, has_side_effects=True, vmem_limit_bytes=56 * MIB
         ),
     )(
         output_gradient,
-        router_weight_table,
-        routes,
+        router_weight_table.T,
+        routes.T,
         hidden[0],
         down_weight_matrix[0],
-        adapter_first_factor[0],
+        adapter_first_factor[0].T,
         adapter_second_factor[0],
     )
-    by_expert = router[:, 0, :].T
-    chosen = routes[:, :, None] == jnp.arange(peers, dtype=jnp.int32)
-    router_weight_gradient = jnp.sum(jnp.where(chosen, by_expert[:, None, :], 0.0), axis=2)
-    return grad[None], first.T[None], second[None], router_weight_gradient
+    return grad[None], first.T[None], second[None], router.T
 
 
 def ring_fits(peers, tokens_dev, width, experts, capacity, inner):
@@ -389,7 +413,7 @@
         and peers >= 8
         and peers % 4 == 0
         and tokens_dev == 128
-        and width % 128 == 0
+        and width % 1024 == 0
         and inner % 128 == 0
         and (2 * per_source) % 16 == 0
         and gathered + inner * width * 2 + 3 * capacity * inner * 2 <= 40 * MIB

time: 116 us -> 109 us (0.940)
  local copies, waits for them, and re-layouts: 9.38 us -> 4.77 us
    unnamed x12 -> x10, local copies, waits for them, and re-layouts: 8.54 us -> 4.77 us
    pallas_call x1, Pallas kernels: 105 us -> 104 us  [ring_shards(): pl.pallas_call(functools.partial(ring_kernel, peers, per_source, strip, p...]
where the time goes in v2:
time: 109 us
  Pallas kernels  104 us (95%)
  local copies, waits for them, and re-layouts  4.77 us (4%)
    pallas_call x1, Pallas kernels, ring_shards(): pl.pallas_call(functools.partial(ring_kernel, peers, per_source, strip, p...  104 us
    unnamed x10, local copies, waits for them, and re-layouts  4.77 us

profile of v2, /device:TPU:0, one launch (start us, length us, event | category | flops | bytes accessed | tf_op | source)
XLA Modules:
  0.0 109.1 jit_solution(4230407241760187956)
XLA Ops:
  0.6 103.7 %shard_map.102 = (bf16[1152,768]{1,0:T(8,128)(2,1)}, f32[16,768]{1,0:T(8,128)}, f32[16,4096]{1,0:T(8,128)}, f32[8,128]{1,0:T(8,128)}) custom-call(bf16[128,4096]{1,0:T(8,128)(2,1)} %grad_hbm.1, bf16[8,128]{1,0:T(8,128)(2,1)} %bitcast.23, s32[8,128]{1,0:T(8,128)} %bitcast.21, bf16[1152,768]{1,0:T(8,128)(2,1)} %bitcast.16, bf16[768,4096]{1,0:T(8,128)(2,1)} %bitcast.14, ...), custom_call_target="tpu_custom_call" | custom-call | tf_op jit(solution)/shard_map/pallas_call | solution.py:358
  104.3 0.0 copy-start.1
  104.3 0.0 copy-start
  104.4 0.0 copy-start.2
  104.4 2.8 %copy.15 = bf16[1,1152,768]{2,1,0:T(8,128)(2,1)} copy(bf16[1,1152,768]{2,1,0:T(8,128)(2,1)} %bitcast.15) | data formatting | bytes 3538944
  107.2 0.0 copy-done.1
  107.2 0.6 copy.16
  107.8 0.0 copy-done
  107.8 0.7 copy.17
  108.5 0.0 copy-done.2
  108.5 0.6 copy.18
Async XLA Ops:
  104.3 2.9 %copy-start.1 = (f32[16,768]{1,0:T(8,128)S(1)}, f32[16,768]{1,0:T(8,128)}, u32[]{:S(2)}) copy-start(f32[16,768]{1,0:T(8,128)} %get-tuple-element.9) | copy-start | bytes 147460
  104.3 3.5 %copy-start = (f32[16,4096]{1,0:T(8,128)S(1)}, f32[16,4096]{1,0:T(8,128)}, u32[]{:S(2)}) copy-start(f32[16,4096]{1,0:T(8,128)} %get-tuple-element.10) | copy-start | bytes 786436
  104.4 4.2 %copy-start.2 = (f32[8,128]{1,0:T(8,128)S(1)}, f32[8,128]{1,0:T(8,128)}, u32[]{:S(2)}) copy-start(f32[8,128]{1,0:T(8,128)} %get-tuple-element.11) | copy-start | bytes 12292

commit v3 on v2

--- a/solution.py
+++ b/solution.py
@@ -38,8 +38,7 @@
     low_in,
     wide,
     thin,
-    meta_out,
-    meta_in,
+    meta,
     router_send,
     router_recv,
     right_send,
@@ -48,8 +47,12 @@
     left_recv,
     pair_send,
     pair_recv,
-    meta_send,
-    meta_got,
+    meta_right_send,
+    meta_right_recv,
+    meta_left_send,
+    meta_left_recv,
+    meta_pair_send,
+    meta_pair_recv,
     back_send,
     back_got,
     local_sem,
@@ -84,8 +87,8 @@
     sibling = chip * 2 + 1 - core
 
     barrier = pltpu.get_barrier_semaphore()
-    for ahead in range(1, peers):
-        pl.semaphore_signal(barrier, inc=1, **device(lax.rem(me + ahead, peers)))
+    for other in (right, left, sibling):
+        pl.semaphore_signal(barrier, inc=1, **device(other))
 
     down_copy = pltpu.make_async_copy(down_hbm, down, local_sem.at[0])
     down_copy.start()
@@ -106,12 +109,9 @@
     earlier = jnp.where(at0 < at1, 1.0, 0.0).astype(jnp.bfloat16)
     before = dot(member.astype(jnp.bfloat16), earlier, (1, 0))
     position = jnp.where(member > 0.5, before, -1.0)
-    meta_out[...] = jnp.zeros_like(meta_out)
-    for e in range(peers):
-        meta_out[e, 0:1, :] = position[e : e + 1, :]
-        meta_out[e, 1:2, :] = weights[e : e + 1, :]
-
-    pl.semaphore_wait(barrier, peers - 1)
+    meta[chip, core] = jnp.concatenate([position, weights], axis=0)
+
+    pl.semaphore_wait(barrier, 3)
 
     def lanes_of(chunk):
         return pl.ds(chunk * piece, piece)
@@ -169,45 +169,37 @@
         block = gathered.at[chip_at(place + 1 + k // parts), at_core, :, lanes_of(parts - 1 - k % parts)]
         return pair_copy(2 + last + k, block)
 
+    def meta_copy(block, send, recv, target):
+        return pltpu.make_async_remote_copy(
+            src_ref=block, dst_ref=block, send_sem=send, recv_sem=recv, **device(target)
+        )
+
+    def meta_right(step, origin):
+        block = meta.at[chip_at(origin), core]
+        return meta_copy(block, meta_right_send.at[step], meta_right_recv.at[step], right)
+
+    def meta_left(step, origin):
+        block = meta.at[chip_at(origin), core]
+        return meta_copy(block, meta_left_send.at[step], meta_left_recv.at[step], left)
+
+    def meta_pair(number, origin, at_core):
+        block = meta.at[chip_at(origin), at_core]
+        return meta_copy(block, meta_pair_send.at[number], meta_pair_recv.at[number], sibling)
+
+    meta_right(0, place).start()
+    meta_left(0, place).start()
+    meta_pair(0, place, core).start()
     for k in range(parts):
         send_right(k).start()
         send_left(k).start()
     own_pair = pair_copy(0, gathered.at[chip, core], grad_hbm)
     own_pair.start()
 
-    def meta_copy(target):
-        return pltpu.make_async_remote_copy(
-            src_ref=meta_out.at[target],
-            dst_ref=meta_in.at[me],
-            send_sem=meta_send.at[target],
-            recv_sem=meta_got.at[me],
-            **device(target),
-        )
-
-    def send_meta(ahead, carry):
-        meta_copy(lax.rem(me + ahead, peers)).start()
-        return carry
-
-    lax.fori_loop(1, peers, send_meta, 0)
-    meta_in[me] = meta_out[me]
-
     first_out[...] = jnp.zeros_like(first_out)
     second_out[...] = jnp.zeros_like(second_out)
     hidden_copy.wait()
     low_in[...] = dot(hidden_ref[...], first_ref[...], (1, 1)).astype(jnp.bfloat16)
 
-    def wait_meta(ahead, carry):
-        source = lax.rem(me + ahead, peers)
-        pltpu.make_async_remote_copy(
-            src_ref=meta_out.at[source],
-            dst_ref=meta_in.at[source],
-            send_sem=meta_send.at[source],
-            recv_sem=meta_got.at[source],
-            **device(source),
-        ).wait()
-        return carry
-
-    lax.fori_loop(1, peers, wait_meta, 0)
     down_copy.wait()
     own_copy.wait()
 
@@ -224,13 +216,18 @@
         where = pl.ds(pl.multiple_of(which * slots, 16), slots)
         return pltpu.make_async_copy(out_ref.at[where, :], out_hbm.at[where, :], out_sem.at[which])
 
-    def work(which):
+    def begin(which):
         where = pl.ds(pl.multiple_of(which * slots, 16), slots)
-        meta0, meta1 = meta_in[2 * which], meta_in[2 * which + 1]
-        high = meta1[0:1, :]
+        mine = lax.broadcasted_iota(jnp.int32, (peers, tokens), 0) == me
+
+        def own_row(at_core, start):
+            table = meta[which, at_core, start : start + peers, :]
+            return jnp.sum(jnp.where(mine, table, 0.0), axis=0, keepdims=True)
+
+        high = own_row(1, 0)
         high = jnp.where(high < 0.0, -1.0, high + float(per_source))
-        slot_of = jnp.concatenate([meta0[0:1, :], high], axis=1)
-        weight = jnp.concatenate([meta0[1:2, :], meta1[1:2, :]], axis=1)
+        slot_of = jnp.concatenate([own_row(0, 0), high], axis=1)
+        weight = jnp.concatenate([own_row(0, peers), own_row(1, peers)], axis=1)
         slot_at = lax.broadcasted_iota(jnp.int32, (slots, 2 * tokens), 0).astype(jnp.float32)
         pick = jnp.where(slot_at == slot_of, 1.0, 0.0)
         slot_weight = jnp.sum(pick * weight, axis=1, keepdims=True)
@@ -242,17 +239,20 @@
         wide[...] = jnp.zeros_like(wide)
         thin[...] = jnp.zeros_like(thin)
 
-        def strip_step(at, carry):
-            lanes = pl.ds(pl.multiple_of(at * strip, strip), strip)
-            block = gathered[which, :, :, lanes].reshape(2 * tokens, strip)
-            product = dot(both, block, (1, 0))
-            slot_rows = product[:slots].astype(jnp.bfloat16)
-            second_out[:, lanes] += adapter_scale * product[slots:]
-            wide[...] += dot(slot_rows, down[:, lanes], (1, 1))
-            thin[...] += dot(slot_rows, second_ref[:, lanes], (1, 1))
-            return carry
-
-        lax.fori_loop(0, width // strip, strip_step, 0)
+        return which, where, hidden, pick, slot_weight, both
+
+    def strip_step(state, at):
+        which, both = state[0], state[-1]
+        lanes = pl.ds(pl.multiple_of(at * strip, strip), strip)
+        block = gathered[which, :, :, lanes].reshape(2 * tokens, strip)
+        product = dot(both, block, (1, 0))
+        slot_rows = product[:slots].astype(jnp.bfloat16)
+        second_out[:, lanes] += adapter_scale * product[slots:]
+        wide[...] += dot(slot_rows, down[:, lanes], (1, 1))
+        thin[...] += dot(slot_rows, second_ref[:, lanes], (1, 1))
+
+    def finish(state):
+        which, where, hidden, pick, slot_weight, _ = state
         low = thin[...]
         total = wide[...] + adapter_scale * dot(low.astype(jnp.bfloat16), first_ref[...], (1, 0))
         out_ref[where, :] = (slot_weight * total).astype(jnp.bfloat16)
@@ -264,20 +264,48 @@
         router_send[2 * which] = jnp.broadcast_to(routed[:, :tokens], (8, tokens))
         router_send[2 * which + 1] = jnp.broadcast_to(routed[:, tokens:], (8, tokens))
 
+    def work(which):
+        state = begin(which)
+
+        def each(at, carry):
+            strip_step(state, at)
+            return carry
+
+        lax.fori_loop(0, parts, each, 0)
+        finish(state)
+
+    def send_back(which):
+        back_copy(2 * which).start()
+        back_copy(2 * which + 1).start()
+
     def work_and_return(which):
         work(which)
-        back_copy(2 * which).start()
-        back_copy(2 * which + 1).start()
+        send_back(which)
 
     def wait_left(step, count):
         for k in range(parts * step, parts * step + count):
             pair_left(k, 1 - core).wait_recv()
+        if count == parts:
+            meta_pair(1 + step, place - 1 - step, 1 - core).wait_recv()
 
     def wait_right(step, count):
         for k in range(parts * step, parts * step + count):
             pair_right(k, 1 - core).wait_recv()
+        if count == parts:
+            meta_pair(1 + far + step, place + 1 + step, 1 - core).wait_recv()
 
     for k in range(last + 1):
+        if k % parts == 0:
+            step = k // parts
+            meta_right(step, place - 1 - step).wait_recv()
+            if step + 1 < far:
+                meta_right(step + 1, place - 1 - step).start()
+            meta_pair(1 + step, place - 1 - step, core).start()
+            if step + 1 < far:
+                meta_left(step, place + 1 + step).wait_recv()
+                if step + 2 < far:
+                    meta_left(step + 1, place + 1 + step).start()
+                meta_pair(1 + far + step, place + 1 + step, core).start()
         from_left(k).wait_recv()
         if k + parts <= last:
             send_right(k + parts).start()
@@ -288,6 +316,7 @@
         pair_right(k, core).start()
         if k == 0:
             pair_copy(0, gathered.at[chip, 1 - core]).wait_recv()
+            meta_pair(0, place, 1 - core).wait_recv()
             work(chip)
             back_copy(sibling).start()
             router_recv[me] = router_send[me]
@@ -300,10 +329,16 @@
                 step = k // parts - 1
             wait_right(step, parts)
             work_and_return(chip_at(place + 1 + step))
-        if k == last:
-            wait_left(far - 1, parts // 2)
-            wait_right(far - 1, parts // 2)
-            work_and_return(chip_at(place + far))
+        if k >= last + 1 - parts // 2:
+            if k == last + 1 - parts // 2:
+                meta_pair(far, place - far, 1 - core).wait_recv()
+                final = begin(chip_at(place + far))
+            pair_left(k, 1 - core).wait_recv()
+            strip_step(final, k % parts)
+            pair_right(k, 1 - core).wait_recv()
+            strip_step(final, parts - 1 - k % parts)
+    finish(final)
+    send_back(chip_at(place + far))
 
     for k in range(last + 1):
         send_right(k).wait_send()
@@ -311,6 +346,13 @@
         pair_left(k, core).wait_send()
         pair_right(k, core).wait_send()
     own_pair.wait_send()
+    meta_pair(0, place, core).wait_send()
+    for step in range(far):
+        meta_right(step, place - step).wait_send()
+        meta_pair(1 + step, place - 1 - step, core).wait_send()
+        if step + 1 < far:
+            meta_left(step, place + step).wait_send()
+            meta_pair(1 + far + step, place + 1 + step, core).wait_send()
 
     def wait_back(ahead, carry):
         source = lax.rem(me + ahead, peers)
@@ -330,6 +372,15 @@
         router_out[k : k + 1, :] = jnp.sum(jnp.where(same, returned, 0.0), axis=0, keepdims=True)
     for which in range(chips):
         out_copy(which).wait()
+
+
+def store_kernel(*refs):
+    sems = refs[8]
+    copies = [pltpu.make_async_copy(refs[i], refs[4 + i], sems.at[i]) for i in range(4)]
+    for copy in copies:
+        copy.start()
+    for copy in copies:
+        copy.wait()
 
 
 def ring_shards(
@@ -350,12 +401,12 @@
     parts = 4
     steps = parts * (chips // 2 - 1) + parts // 2
     top = routes.shape[1]
-    strip = 1024
+    strip = width // parts
     vmem = pl.BlockSpec(memory_space=pltpu.VMEM)
     hbm = pl.BlockSpec(memory_space=pl.ANY)
     dma = pltpu.SemaphoreType.DMA
     small = (peers, 8, tokens)
-    grad, first, second, router = pl.pallas_call(
+    results = pl.pallas_call(
         functools.partial(ring_kernel, peers, per_source, strip, parts),
         out_shape=(
             jax.ShapeDtypeStruct((capacity, inner), jnp.bfloat16),
@@ -373,8 +424,7 @@
             pltpu.VMEM((capacity, rank), jnp.bfloat16),
             pltpu.VMEM((2 * per_source, inner), jnp.float32),
             pltpu.VMEM((2 * per_source, rank), jnp.float32),
-            pltpu.VMEM(small, jnp.float32),
-            pltpu.VMEM(small, jnp.float32),
+            pltpu.VMEM((chips, 2, 2 * peers, tokens), jnp.float32),
             pltpu.VMEM(small, jnp.float32),
             pltpu.VMEM(small, jnp.float32),
             dma((steps,)),
@@ -383,8 +433,12 @@
             dma((steps,)),
             dma((2 * steps + 1,)),
             dma((2 * steps + 1,)),
-            dma((peers,)),
-            dma((peers,)),
+            dma((chips // 2,)),
+            dma((chips // 2,)),
+            dma((chips // 2,)),
+            dma((chips // 2,)),
+            dma((chips,)),
+            dma((chips,)),
             dma((peers,)),
             dma((peers,)),
             dma((3,)),
@@ -402,6 +456,13 @@
         adapter_first_factor[0].T,
         adapter_second_factor[0],
     )
+    grad, first, second, router = pl.pallas_call(
+        store_kernel,
+        out_shape=[jax.ShapeDtypeStruct(r.shape, r.dtype) for r in results],
+        in_specs=[vmem] * 4,
+        out_specs=[hbm] * 4,
+        scratch_shapes=[dma((4,))],
+    )(*results)
     return grad[None], first.T[None], second[None], router.T
 
 
@@ -413,7 +474,7 @@
         and peers >= 8
         and peers % 4 == 0
         and tokens_dev == 128
-        and width % 1024 == 0
+        and width % 512 == 0
         and inner % 128 == 0
         and (2 * per_source) % 16 == 0
         and gathered + inner * width * 2 + 3 * capacity * inner * 2 <= 40 * MIB

time: 109 us -> 101 us (0.927)
  local copies, waits for them, and re-layouts: 4.77 us -> 0 us
  Pallas kernels: 104 us -> 101 us
    pallas_call x1, Pallas kernels: 104 us -> 97.8 us  [ring_shards(): pl.pallas_call(functools.partial(ring_kernel, peers, per_source, strip, p...]
    unnamed x10 -> x0, local copies, waits for them, and re-layouts: 4.77 us -> none
    pallas_call x0 -> x1, Pallas kernels: none -> 2.85 us  [ring_shards(): pl.pallas_call(store_kernel, out_shape=[jax.ShapeDtypeStruct(r.shape, r.d...]
where the time goes in v3:
time: 101 us
  Pallas kernels  101 us (100%)
    pallas_call x1, Pallas kernels, ring_shards(): pl.pallas_call(functools.partial(ring_kernel, peers, per_source, strip, p...  97.8 us
    pallas_call x1, Pallas kernels, ring_shards(): pl.pallas_call(store_kernel, out_shape=[jax.ShapeDtypeStruct(r.shape, r.d...  2.85 us

profile of v3, /device:TPU:0, one launch (start us, length us, event | category | flops | bytes accessed | tf_op | source)
XLA Modules:
  0.0 101.3 jit_solution(762929887983004956)
XLA Ops:
  0.6 97.8 %shard_map.102 = (bf16[1152,768]{1,0:T(8,128)(2,1)}, f32[16,768]{1,0:T(8,128)}, f32[16,4096]{1,0:T(8,128)}, f32[8,128]{1,0:T(8,128)}) custom-call(bf16[128,4096]{1,0:T(8,128)(2,1)} %grad_hbm.1, bf16[8,128]{1,0:T(8,128)(2,1)} %bitcast.19, s32[8,128]{1,0:T(8,128)} %bitcast.18, bf16[1152,768]{1,0:T(8,128)(2,1)} %bitcast.15, bf16[768,4096]{1,0:T(8,128)(2,1)} %bitcast.14, ...), custom_call_target="tpu_custom_call" | custom-call | tf_op jit(solution)/shard_map/pallas_call | solution.py:409
  98.4 2.9 %shard_map.103 = (bf16[1152,768]{1,0:T(8,128)(2,1)}, f32[16,768]{1,0:T(8,128)}, f32[16,4096]{1,0:T(8,128)}, f32[8,128]{1,0:T(8,128)}) custom-call(bf16[1152,768]{1,0:T(8,128)(2,1)} %get-tuple-element.12.refs_0_, f32[16,768]{1,0:T(8,128)} %get-tuple-element.13.refs_1_, f32[16,4096]{1,0:T(8,128)} %get-tuple-element.14.refs_2_, f32[8,128]{1,0:T(8,128)} %get-tuple-element.15.refs_3_), custom_call_target="tpu_custom_call" | custom-call | tf_op jit(solution)/shard_map/pallas_call | solution.py:459

commit v4 on v3

--- a/solution.py
+++ b/solution.py
@@ -216,6 +216,10 @@
         where = pl.ds(pl.multiple_of(which * slots, 16), slots)
         return pltpu.make_async_copy(out_ref.at[where, :], out_hbm.at[where, :], out_sem.at[which])
 
+    def send_back(which):
+        back_copy(2 * which).start()
+        back_copy(2 * which + 1).start()
+
     def begin(which):
         where = pl.ds(pl.multiple_of(which * slots, 16), slots)
         mine = lax.broadcasted_iota(jnp.int32, (peers, tokens), 0) == me
@@ -251,20 +255,25 @@
         wide[...] += dot(slot_rows, down[:, lanes], (1, 1))
         thin[...] += dot(slot_rows, second_ref[:, lanes], (1, 1))
 
-    def finish(state):
+    def finish(state, own=False):
         which, where, hidden, pick, slot_weight, _ = state
         low = thin[...]
         total = wide[...] + adapter_scale * dot(low.astype(jnp.bfloat16), first_ref[...], (1, 0))
+        router = jnp.sum(hidden.astype(jnp.float32) * total, axis=1, keepdims=True)
+        routed = jnp.sum(pick * router, axis=0, keepdims=True)
+        router_send[2 * which] = jnp.broadcast_to(routed[:, :tokens], (8, tokens))
+        router_send[2 * which + 1] = jnp.broadcast_to(routed[:, tokens:], (8, tokens))
+        if own:
+            back_copy(sibling).start()
+            router_recv[me] = router_send[me]
+        else:
+            send_back(which)
         out_ref[where, :] = (slot_weight * total).astype(jnp.bfloat16)
         out_copy(which).start()
         low_grad = (slot_weight * low).astype(jnp.bfloat16)
         first_out[...] += adapter_scale * dot(low_grad, hidden, (0, 0))
-        router = jnp.sum(hidden.astype(jnp.float32) * total, axis=1, keepdims=True)
-        routed = jnp.sum(pick * router, axis=0, keepdims=True)
-        router_send[2 * which] = jnp.broadcast_to(routed[:, :tokens], (8, tokens))
-        router_send[2 * which + 1] = jnp.broadcast_to(routed[:, tokens:], (8, tokens))
-
-    def work(which):
+
+    def work(which, own=False):
         state = begin(which)
 
         def each(at, carry):
@@ -272,15 +281,7 @@
             return carry
 
         lax.fori_loop(0, parts, each, 0)
-        finish(state)
-
-    def send_back(which):
-        back_copy(2 * which).start()
-        back_copy(2 * which + 1).start()
-
-    def work_and_return(which):
-        work(which)
-        send_back(which)
+        finish(state, own)
 
     def wait_left(step, count):
         for k in range(parts * step, parts * step + count):
@@ -293,6 +294,10 @@
             pair_right(k, 1 - core).wait_recv()
         if count == parts:
             meta_pair(1 + far + step, place + 1 + step, 1 - core).wait_recv()
+
+    pair_copy(0, gathered.at[chip, 1 - core]).wait_recv()
+    meta_pair(0, place, 1 - core).wait_recv()
+    work(chip, own=True)
 
     for k in range(last + 1):
         if k % parts == 0:
@@ -314,21 +319,15 @@
         if k + parts <= last:
             send_left(k + parts).start()
         pair_right(k, core).start()
-        if k == 0:
-            pair_copy(0, gathered.at[chip, 1 - core]).wait_recv()
-            meta_pair(0, place, 1 - core).wait_recv()
-            work(chip)
-            back_copy(sibling).start()
-            router_recv[me] = router_send[me]
         step = (k + 1) // parts - 1
         if k % parts == parts - 1:
             wait_left(step, parts)
-            work_and_return(chip_at(place - 1 - step))
+            work(chip_at(place - 1 - step))
         if (k % parts == 0 and k > 0 and k < last) or (k + 1 == last and k % parts == parts - 1):
             if k % parts == 0:
                 step = k // parts - 1
             wait_right(step, parts)
-            work_and_return(chip_at(place + 1 + step))
+            work(chip_at(place + 1 + step))
         if k >= last + 1 - parts // 2:
             if k == last + 1 - parts // 2:
                 meta_pair(far, place - far, 1 - core).wait_recv()
@@ -338,7 +337,6 @@
             pair_right(k, 1 - core).wait_recv()
             strip_step(final, parts - 1 - k % parts)
     finish(final)
-    send_back(chip_at(place + far))
 
     for k in range(last + 1):
         send_right(k).wait_send()

time: 101 us -> 101 us (level)
  no operation moved by 1% of the time
where the time goes in v4:
time: 101 us
  Pallas kernels  101 us (100%)
    pallas_call x1, Pallas kernels, ring_shards(): pl.pallas_call(functools.partial(ring_kernel, peers, per_source, strip, p...  97.8 us
    pallas_call x1, Pallas kernels, ring_shards(): pl.pallas_call(store_kernel, out_shape=[jax.ShapeDtypeStruct(r.shape, r.d...  2.85 us

profile of v4, /device:TPU:0, one launch (start us, length us, event | category | flops | bytes accessed | tf_op | source)
XLA Modules:
  0.0 101.3 jit_solution(3976192966582347449)
XLA Ops:
  0.6 97.8 %shard_map.102 = (bf16[1152,768]{1,0:T(8,128)(2,1)}, f32[16,768]{1,0:T(8,128)}, f32[16,4096]{1,0:T(8,128)}, f32[8,128]{1,0:T(8,128)}) custom-call(bf16[128,4096]{1,0:T(8,128)(2,1)} %grad_hbm.1, bf16[8,128]{1,0:T(8,128)(2,1)} %bitcast.19, s32[8,128]{1,0:T(8,128)} %bitcast.18, bf16[1152,768]{1,0:T(8,128)(2,1)} %bitcast.15, bf16[768,4096]{1,0:T(8,128)(2,1)} %bitcast.14, ...), custom_call_target="tpu_custom_call" | custom-call | tf_op jit(solution)/shard_map/pallas_call | solution.py:407
  98.4 2.9 %shard_map.103 = (bf16[1152,768]{1,0:T(8,128)(2,1)}, f32[16,768]{1,0:T(8,128)}, f32[16,4096]{1,0:T(8,128)}, f32[8,128]{1,0:T(8,128)}) custom-call(bf16[1152,768]{1,0:T(8,128)(2,1)} %get-tuple-element.12.refs_0_, f32[16,768]{1,0:T(8,128)} %get-tuple-element.13.refs_1_, f32[16,4096]{1,0:T(8,128)} %get-tuple-element.14.refs_2_, f32[8,128]{1,0:T(8,128)} %get-tuple-element.15.refs_3_), custom_call_target="tpu_custom_call" | custom-call | tf_op jit(solution)/shard_map/pallas_call | solution.py:457
